TPU v7x, 32 devices: a whole 2x2x4 slice. The times are simulated.
32 devices in a mesh: lat: 4 (over y, x), lon: 4 (over z), feat: 2 (over core).
Axes of the slice: x: 2, y: 2, z: 4, core: 2. Of those that a mesh axis runs over, the one named last changes fastest.
Arguments:
- atmosphere: float32 [384, 768, 256], P('lat', 'lon', 'feat'), may hold values from -6 to 6
- spectral_weight: float32 [2, 384, 256, 256], P(None, ('lat', 'lon'), None, 'feat'), may hold values from -0.25 to 0.25
- mlp_in: float32 [256, 768], P(None, 'feat'), may hold values from -0.375 to 0.375
- mlp_out: float32 [768, 256], P(None, 'feat'), may hold values from -0.21875 to 0.21875
- ocean_state: float32 [256, 64, 256], P('lat', 'lon', 'feat'), may hold values from -6 to 6
- depth_kernel: float32 [7, 7, 256], P(None, None, 'feat'), may hold values from -0.875 to 0.875
- depth_bias: float32 [256], P('feat'), may hold values from -4 to 4
- norm_gain: float32 [256], replicated, may hold values from 0.5 to 1.5
- ocean_up: float32 [256, 1024], P(None, 'feat'), may hold values from -0.375 to 0.375
- ocean_down: float32 [1024, 256], P(None, 'feat'), may hold values from -0.1875 to 0.1875
- ocean_bias: float32 [256], P('feat'), may hold values from -3 to 3
- layer_scale: float32 [256], P('feat'), may hold values from 0.5 to 1.5
- flux_weight: float32 [256, 256], P(None, 'feat'), may hold values from -0.375 to 0.375
- regrid_rows: int32 [4, 4, 4, 256], P('lat', 'lon'), may hold values from 0 to 18431
- ocean_rows: int32 [256, 64], P('lat', 'lon'), may hold values from 0 to 1023
- land_mask: int32 [32, 8], P('lat', 'lon'), may hold values 0 or 1
Outputs:
- atmos_next: float32 [384, 768, 256], P('lat', 'lon', 'feat')
- ocean_next: float32 [256, 64, 256], P('lat', 'lon', 'feat')
Inputs may be any that keep to these rules, and one draw needn't show every extreme that they name: regrid_rows[a, s, b, k] counts the points of latitude band a and longitude sector s latitude-major, 192 to a latitude. ocean_rows[i, o] = s * 256 + k names the k-th point that the cell's tile takes from sector s. `land_mask`: 1 for a sea block, 0 for a land block.
All inputs are finite; a program needn't handle non-finite values.
Results may differ from a plain program's by a relative error of at most 0.0003.
Values sent between devices are 32-bit elements; how exact they have to be, the bound alone decides.
A program may use at most 192 MiB of HBM per device.

v0:
```python
import math

import jax
import jax.numpy as jnp
from jax import lax
from jax.sharding import PartitionSpec as P

C = 256
NLAT = 384
NLON = 768
LMAX = 384
MMAX = 256
KERNEL = 7
BLOCK = 8


best_precision = lax.Precision.HIGHEST


def with_halo(block, sides, width):
    for axis, dim in sides:
        count = lax.axis_size(axis)
        forward = [(i, i + 1) for i in range(count - 1)]
        backward = [(target, source) for source, target in forward]
        low = lax.ppermute(
            lax.slice_in_dim(block, block.shape[dim] - width, None, axis=dim), axis, forward
        )
        high = lax.ppermute(lax.slice_in_dim(block, 0, width, axis=dim), axis, backward)
        block = jnp.concatenate([low, block, high], axis=dim)
    return block


def legendre_table(orders, degree_count, lat_count, order_limit):
    index_lat = jnp.arange(lat_count, dtype=jnp.int32).astype(jnp.float32)
    colat = math.pi * (index_lat + 0.5) / lat_count
    cosine = jnp.cos(colat)
    sine = jnp.sin(colat)
    order_f = orders.astype(jnp.float32)[:, None]
    steps_k = jnp.arange(1, order_limit + 1, dtype=jnp.int32)
    step_f = steps_k.astype(jnp.float32)
    log_terms = jnp.log((2.0 * step_f + 1.0) / (2.0 * step_f))
    log_norm = jnp.sum(
        jnp.where(steps_k[None, :] <= orders[:, None], log_terms[None, :], 0.0), axis=1
    )
    log_start = 0.5 * (math.log(0.5) + log_norm[:, None]) + order_f * jnp.log(sine)[None, :]
    zeros_grid = jnp.zeros((orders.shape[0], lat_count), jnp.float32)

    def advance(carry, degree):
        current, previous, shift = carry
        deg_f = degree.astype(jnp.float32)
        order_sq = order_f * order_f
        factor_a = jnp.sqrt(
            jnp.maximum(4.0 * deg_f * deg_f - 1.0, 0.0) / jnp.maximum(deg_f * deg_f - order_sq, 1.0)
        )
        below = deg_f - 1.0
        factor_b = jnp.sqrt(
            jnp.maximum(below * below - order_sq, 0.0) / jnp.maximum(4.0 * below * below - 1.0, 1.0)
        )
        recurred = factor_a * (cosine[None, :] * current - factor_b * previous)
        fresh = jnp.where(
            degree == orders[:, None], 1.0, jnp.where(degree > orders[:, None], recurred, 0.0)
        )
        large = jnp.abs(fresh) > 2.0**32
        rescale = jnp.where(large, 2.0 ** (-32), 1.0)
        fresh = fresh * rescale
        shift = shift + jnp.where(large, 32.0, 0.0)
        value = fresh * jnp.exp(log_start + shift * math.log(2.0))
        return ((fresh, current * rescale, shift), value)

    final_state, table = lax.scan(
        advance,
        (zeros_grid, zeros_grid, zeros_grid),
        jnp.arange(degree_count, dtype=jnp.int32),
        unroll=16,
    )
    return table


def quadrature(lat_ids, lat_count):
    colat = math.pi * (lat_ids.astype(jnp.float32) + 0.5) / lat_count
    return jnp.sin(colat) * (math.pi / lat_count)


def forward_table(lon_count, order_count):
    lon_ids = jnp.arange(lon_count, dtype=jnp.int32)[:, None]
    order_ids = jnp.arange(order_count, dtype=jnp.int32)[None, :]
    phase = 2.0 * math.pi / lon_count * (lon_ids * order_ids % lon_count).astype(jnp.float32)
    return jnp.stack([jnp.cos(phase), -jnp.sin(phase)], axis=0) / lon_count


def inverse_table(lon_count, order_count):
    order_ids = jnp.arange(order_count, dtype=jnp.int32)[:, None]
    lon_ids = jnp.arange(lon_count, dtype=jnp.int32)[None, :]
    phase = 2.0 * math.pi / lon_count * (order_ids * lon_ids % lon_count).astype(jnp.float32)
    weight = jnp.where(order_ids == 0, 1.0, 2.0)
    return jnp.stack([jnp.cos(phase) * weight, -jnp.sin(phase) * weight], axis=0)


def regroup(blocks):
    return lax.all_to_all(blocks, "lon", split_axis=0, concat_axis=2, tiled=True)[0]


def band_exchange(blocks):
    return lax.all_to_all(blocks, "lat", split_axis=0, concat_axis=2, tiled=True)


def degree_exchange(blocks):
    return lax.all_to_all(blocks, ("lat", "lon"), split_axis=0, concat_axis=2, tiled=True)


def channel_join(matrix):
    return lax.all_gather(matrix, "feat", axis=1, tiled=True)


def feed_forward(inputs, up_weight, down_weight):
    whole_up = channel_join(up_weight)
    hidden = jax.nn.gelu(
        jnp.dot(inputs, whole_up, precision=best_precision, preferred_element_type=jnp.float32),
        approximate=False,
    )
    return jnp.dot(
        hidden, down_weight, precision=best_precision, preferred_element_type=jnp.float32
    )


def shards(
    atmosphere,
    spectral_weight,
    mlp_in,
    mlp_out,
    ocean_state,
    depth_kernel,
    depth_bias,
    norm_gain,
    ocean_up,
    ocean_down,
    ocean_bias,
    layer_scale,
    flux_weight,
    regrid_rows,
    ocean_rows,
    land_mask,
):
    lat_rows, lon_cols, half_chan = atmosphere.shape
    lon_devices = lax.axis_size("lon")
    lat_devices = lax.axis_size("lat")
    lat_index = lax.axis_index("lat")
    lon_index = lax.axis_index("lon")
    band_rows = lat_rows // lon_devices
    order_local = MMAX // lon_devices
    degree_rows = LMAX // lat_devices
    mix_rows = degree_rows // lon_devices
    few_orders = order_local // lat_devices
    flat_atm = atmosphere.reshape(-1, half_chan)
    picked = jnp.take(flat_atm, regrid_rows.reshape(-1), axis=0).reshape(lon_devices, -1, half_chan)
    arrived = lax.all_to_all(picked, "lon", split_axis=0, concat_axis=0, tiled=True)
    grid = regroup(atmosphere.reshape(lon_devices, band_rows, lon_cols, half_chan))
    spectrum = jnp.einsum(
        "anc,rnm->mrac", grid, forward_table(NLON, MMAX), precision=best_precision
    )
    spectrum = regroup(spectrum.reshape(lon_devices, order_local * 2, band_rows, half_chan))
    spectrum = spectrum.reshape(order_local, 2, lat_rows, half_chan)
    spread = band_exchange(spectrum)
    orders = (
        lon_index * order_local + lat_index * few_orders + jnp.arange(few_orders, dtype=jnp.int32)
    )
    table = legendre_table(orders, LMAX, NLAT, MMAX)
    quad = quadrature(jnp.arange(NLAT, dtype=jnp.int32), NLAT)
    coeffs = jnp.einsum(
        "lmj,mrjc->lrmc", table * quad[None, None, :], spread, precision=best_precision
    )
    mix_flat = degree_exchange(coeffs).reshape(-1, half_chan)
    mix_input = channel_join(mix_flat).reshape(mix_rows, 2, MMAX, C)
    real_part = jnp.einsum(
        "lmc,lcd->mld", mix_input[:, 0], spectral_weight[0], precision=best_precision
    ) - jnp.einsum("lmc,lcd->mld", mix_input[:, 1], spectral_weight[1], precision=best_precision)
    imag_part = jnp.einsum(
        "lmc,lcd->mld", mix_input[:, 1], spectral_weight[0], precision=best_precision
    ) + jnp.einsum("lmc,lcd->mld", mix_input[:, 0], spectral_weight[1], precision=best_precision)
    mixed = jnp.stack([real_part, imag_part], axis=1)
    back = degree_exchange(mixed)
    full_modes = jnp.einsum("lmj,mrlc->jrmc", table, back, precision=best_precision)
    grid_modes = band_exchange(full_modes)
    wave_rows = regroup(grid_modes.reshape(lon_devices, band_rows * 2, order_local, half_chan))
    wave_rows = wave_rows.reshape(band_rows, 2, MMAX, half_chan)
    spatial = jnp.einsum(
        "armc,rmn->nac", wave_rows, inverse_table(NLON, MMAX), precision=best_precision
    )
    spatial = regroup(spatial.reshape(lon_devices, lon_cols, band_rows, half_chan))
    summed = atmosphere + jnp.transpose(spatial, (1, 0, 2))
    full_input = channel_join(summed.reshape(-1, half_chan))
    atm_update = feed_forward(full_input, mlp_in, mlp_out)
    atmos_next = summed + atm_update.reshape(lat_rows, lon_cols, half_chan)
    tile_rows, tile_cols, ocean_half = ocean_state.shape
    padded = with_halo(ocean_state, (("lat", 0), ("lon", 1)), KERNEL // 2)
    conv = jnp.zeros((tile_rows, tile_cols, ocean_half), jnp.float32) + depth_bias
    for tap_row in range(KERNEL):
        for tap_col in range(KERNEL):
            conv = (
                conv
                + padded[tap_row : tap_row + tile_rows, tap_col : tap_col + tile_cols]
                * depth_kernel[tap_row, tap_col]
            )
    arrived_full = channel_join(arrived.reshape(-1, half_chan))
    flux_rows = jnp.dot(
        arrived_full, flux_weight, precision=best_precision, preferred_element_type=jnp.float32
    )
    forcing = jnp.take(flux_rows, ocean_rows.reshape(-1), axis=0).reshape(
        tile_rows, tile_cols, ocean_half
    )
    joined = conv + forcing
    full_rows = channel_join(joined.reshape(-1, ocean_half))
    row_mean = jnp.mean(full_rows, axis=-1, keepdims=True)
    centered = full_rows - row_mean
    variance = jnp.mean(centered * centered, axis=-1, keepdims=True)
    normed = centered * lax.rsqrt(variance + 1e-06) * norm_gain
    update = feed_forward(normed, ocean_up, ocean_down) + ocean_bias
    mask_rows = tile_rows // BLOCK
    mask_cols = tile_cols // BLOCK
    cell_mask = (
        jnp.broadcast_to(land_mask[:, None, :, None], (mask_rows, BLOCK, mask_cols, BLOCK))
        .reshape(tile_rows, tile_cols)
        .astype(jnp.float32)
    )
    ocean_next = ocean_state + cell_mask[:, :, None] * layer_scale * update.reshape(
        tile_rows, tile_cols, ocean_half
    )
    return (atmos_next, ocean_next)


def solution(mesh):
    in_specs = (
        P("lat", "lon", "feat"),
        P(None, ("lat", "lon"), None, "feat"),
        P(None, "feat"),
        P(None, "feat"),
        P("lat", "lon", "feat"),
        P(None, None, "feat"),
        P("feat"),
        P(),
        P(None, "feat"),
        P(None, "feat"),
        P("feat"),
        P("feat"),
        P(None, "feat"),
        P("lat", "lon", None, None),
        P("lat", "lon"),
        P("lat", "lon"),
    )
    out_specs = (P("lat", "lon", "feat"), P("lat", "lon", "feat"))
    return jax.shard_map(shards, mesh=mesh, in_specs=in_specs, out_specs=out_specs, check_vma=False)
```

profile of v0, /device:TPU:0, one launch (start us, length us, event | category | flops | bytes accessed | tf_op | source)
XLA Modules:
  0.0 2200.6 jit_solution(13574059113698341629)
XLA Ops:
  7.2 6.5 all-to-all-start
  13.6 3.2 sine_negate_fusion
  16.8 203.6 %all-to-all-done = f32[4,24,192,128]{3,2,1,0:T(8,128)} async-done(((f32[4,24,192,128]{3,2,1,0:T(8,128)}), f32[4,24,192,128]{3,2,1,0:T(8,128)}, u32[]{:S(2)}, u32[]{:S(2)}) %all-to-all-start) | async-done | bytes 9437216 | tf_op jit(solution)/shard_map/all_to_all | solution.py:100
  220.4 4.3 copy.89
  224.7 16.0 convolution_bitcast_fusion.1
  240.8 6.2 copy.90
  247.0 5.3 all-to-all-start.1
  252.7 137.5 %all-to-all-done.1 = f32[4,128,24,128]{3,2,1,0:T(8,128)} async-done(((f32[4,128,24,128]{3,2,1,0:T(8,128)}), f32[4,128,24,128]{3,2,1,0:T(8,128)}, u32[]{:S(2)}, u32[]{:S(2)}) %all-to-all-start.1) | async-done | bytes 6291488 | tf_op jit(solution)/shard_map/all_to_all | solution.py:100
  390.2 6.3 copy.91
  396.5 5.3 all-to-all-start.2
  401.8 594.5 %while.23 = (s32[]{:T(128)}, f32[16,384]{1,0:T(8,128)S(1)}, f32[16,384]{1,0:T(8,128)S(1)}, f32[16,384]{1,0:T(8,128)S(1)}, f32[24,16,16,384]{3,2,1,0:T(8,128)}, /...) while((s32[]{:T(128)}, f32[16,384]{1,0:T(8,128)S(1)}, ...), condition=%wide.region_2.3_spmd.clone.clone.clone.clone, body=%wide.region_1.2_spmd.clone.clone.clone.clone.sunk | while | flops 4311377 | bytes 3016219 | solution.py:70
  996.4 3.6 copy.92
  1000.0 1.9 copy-done.3
  1001.9 24.4 %fusion.335 = f32[384,2,16,128]{0,3,1,2:T(8,128)} fusion(f32[16,2,384,128]{3,2,1,0:T(8,128)S(1)} %bitcast.468, f32[384,16,384]{2,1,0:T(8,128)S(1)} %bitcast.462, f32[384]{0:T(512)S(1)} %fusion.531), kind=kOutput, calls=%fused_computation.509 | convolution fusion | flops 7250116608 | bytes 22021632 | tf_op jit(solution)/shard_map/lmj,mrjc->lrmc/dot_general | solution.py:169
  1026.3 10.2 copy.95
  1036.5 143.5 %all_to_all.131 = f32[384,2,16,128]{3,1,2,0:T(2,128)S(1)} all-to-all(f32[384,2,16,128]{3,1,2,0:T(2,128)} %copy.95), channel_id=1, replica_groups=mesh['lat'=4,'lon'=4,'feat'=2] {'lat','lon'}, dimensions={0} | all-to-all | bytes 12582912 | tf_op jit(solution)/shard_map/all_to_all | solution.py:108
  1180.7 3.5 copy.97
  1184.2 22.3 %all-gather.6.cloned.1.call-done = f32[12288,256]{1,0:T(8,128)} async-done(((f32[12288,128]{1,0:T(8,128)}), f32[12288,256]{1,0:T(8,128)}) %all-gather.6.cloned.1.call-update) | async-done | bytes 12582928 | tf_op jit(solution)/shard_map/all_gather | solution.py:112
  1206.5 10.4 fusion.260
  1216.9 8.2 fusion.261
  1225.2 6.3 add_bitcast_fusion
  1231.5 6.5 subtract_bitcast_fusion
  1238.7 3.6 copy.100
  1242.4 147.3 %all_to_all.132 = f32[256,2,24,128]{3,2,1,0:T(8,128)S(1)} all-to-all(f32[256,2,24,128]{3,2,1,0:T(8,128)S(1)} %copy.100), channel_id=1, replica_groups=mesh['lat'=4,'lon'=4,'feat'=2] {'lat','lon'}, dimensions={0} | all-to-all | bytes 12582912 | tf_op jit(solution)/shard_map/all_to_all | solution.py:108
  1390.9 16.0 fusion.332
  1406.9 10.3 copy.104
  1417.2 73.6 %all_to_all.133 = f32[384,2,16,128]{3,1,2,0:T(2,128)S(1)} all-to-all(f32[384,2,16,128]{3,1,2,0:T(2,128)} %copy.104), channel_id=1, replica_groups=mesh['lat'=4,'lon'=4,'feat'=2] {'lat'}, dimensions={0} | all-to-all | bytes 12582912 | tf_op jit(solution)/shard_map/all_to_all | solution.py:104
  1491.5 3.6 copy.106
  1495.0 5.4 all-to-all-start.6
  1500.5 6.5 gather_fusion
  1507.0 1.0 broadcast_select_fusion
  1508.0 3.3 cosine_multiply_fusion
  1511.2 125.3 %all-to-all-done.6 = f32[4,48,64,128]{3,2,1,0:T(8,128)} async-done(((f32[4,48,64,128]{3,2,1,0:T(8,128)}), f32[4,48,64,128]{3,2,1,0:T(8,128)}, u32[]{:S(2)}, u32[]{:S(2)}) %all-to-all-start.6) | async-done | bytes 6291488 | tf_op jit(solution)/shard_map/all_to_all | solution.py:100
  1636.6 3.9 all-to-all-start.8
  1640.6 3.4 copy.107
  1643.9 18.0 convolution_bitcast_fusion
  1661.9 0.8 copy-done.5
  1662.7 5.8 all-to-all-start.7
  1668.6 3.2 collective-permute-start
  1671.7 1.3 collective-permute-start.1
  1674.9 2.6 collective-permute-done.1
  1677.5 0.8 copy-done.6
  1678.4 1.3 collective-permute-start.3
  1679.7 5.2 collective-permute-start.2
  1684.9 1.5 all-gather.10.cloned.1.call-done
  1686.4 2.2 fusion.607
  1688.6 3.0 gather_fusion.1
  1691.6 84.1 %collective-permute-done.3 = f32[70,3,128]{2,1,0:T(4,128)} collective-permute-done((f32[70,3,128]{2,1,0:T(4,128)S(1)}, f32[70,3,128]{2,1,0:T(4,128)}, u32[]{:S(2)}, u32[]{:S(2)}) %collective-permute-start.3) | collective-permute-done | bytes 107552 | tf_op jit(solution)/shard_map/ppermute | solution.py:28
  1775.7 47.2 %collective-permute-done.2 = f32[70,3,128]{2,1,0:T(4,128)} collective-permute-done((f32[70,3,128]{2,1,0:T(4,128)S(1)}, f32[70,3,128]{2,1,0:T(4,128)}, u32[]{:S(2)}, u32[]{:S(2)}) %collective-permute-start.2) | collective-permute-done | bytes 107552 | tf_op jit(solution)/shard_map/ppermute | solution.py:25
  1822.9 19.5 fusion.400
  1843.0 31.6 %all-to-all-done.7 = f32[4,192,24,128]{3,1,2,0:T(8,128)} async-done(((f32[4,192,24,128]{3,1,2,0:T(8,128)}), f32[4,192,24,128]{3,1,2,0:T(8,128)}, u32[]{:S(2)}, u32[]{:S(2)}) %all-to-all-start.7) | async-done | bytes 9437216 | tf_op jit(solution)/shard_map/all_to_all | solution.py:100
  1874.7 13.0 bitcast_add_fusion
  1888.7 2.8 all_gather.20
  1891.5 10.9 all-gather.12.cloned.1.call-done
  1902.4 1.4 reduce_sum.28
  1903.8 1.6 multiply_reduce_fusion
  1905.4 8.6 all-gather.14.cloned.1.call-done
  1914.0 5.4 fusion.380
  1919.4 12.5 fusion.377
  1932.0 1.0 multiply_add_fusion.1
  1933.0 18.0 all-gather.8.cloned.1.call-done
  1951.0 52.5 %fusion.606 = f32[18432,768]{1,0:T(8,128)} fusion(f32[18432,256]{1,0:T(8,128)} %all-gather.8.cloned.1.call-done, f32[256,768]{1,0:T(8,128)S(1)} %all_gather.20), kind=kOutput, calls=%fused_computation.899 | convolution fusion | flops 43486543872 | bytes 76283904 | tf_op jit(solution)/shard_map/dot_general | solution.py:118
  2003.5 177.4 %fusion.169 = f32[18432,128]{1,0:T(8,128)} fusion(f32[768,128]{1,0:T(8,128)S(1)} %copy-done.14, f32[18432,768]{1,0:T(8,128)} %fusion.606), kind=kOutput, calls=%fused_computation.287 | convolution fusion | flops 22649241600 | bytes 66453504 | tf_op jit(solution)/shard_map/dot_general | solution.py:121
  2180.9 13.0 add.871
  (1344 shorter events, 343.0 us)
Async XLA Ops:
  7.2 1912.2 %copy-start = (f32[1024,128]{1,0:T(8,128)S(1)}, f32[1024,128]{1,0:T(8,128)}, u32[]{:S(2)}) copy-start(f32[1024,128]{1,0:T(8,128)} %param.27) | copy-start | bytes 1572868
  7.2 213.2 %all-to-all-start = ((f32[4,24,192,128]{3,2,1,0:T(8,128)}), f32[4,24,192,128]{3,2,1,0:T(8,128)}, u32[]{:S(2)}, u32[]{:S(2)}) async-start(f32[4,24,192,128]{3,2,1,0:T(8,128)} %bitcast.455), calls=%async_computation | async-start | bytes 18874368 | tf_op jit(solution)/shard_map/all_to_all | solution.py:100
  247.0 143.2 %all-to-all-start.1 = ((f32[4,128,24,128]{3,2,1,0:T(8,128)}), f32[4,128,24,128]{3,2,1,0:T(8,128)}, u32[]{:S(2)}, u32[]{:S(2)}) async-start(f32[4,128,24,128]{3,2,1,0:T(8,128)} %bitcast.470), calls=%async_computation.1 | async-start | bytes 12582912 | tf_op jit(solution)/shard_map/all_to_all | solution.py:100
  396.5 599.9 %all-to-all-start.2 = ((f32[64,2,96,128]{3,2,1,0:T(8,128)}), f32[64,2,96,128]{3,2,1,0:T(8,128)}, u32[]{:S(2)}, u32[]{:S(2)}) async-start(f32[64,2,96,128]{3,2,1,0:T(8,128)} %bitcast.469), calls=%async_computation.2 | async-start | bytes 12582912 | tf_op jit(solution)/shard_map/all_to_all | solution.py:104
  401.8 804.7 %all-gather.6.cloned.1.call-start = ((), (), s32[]{:S(2)}) async-start(), calls=%async_computation.9 | async-start | bytes 18874368 | tf_op jit(solution)/shard_map/all_gather | solution.py:112
  996.4 5.5 copy-start.3
  1206.5 10.4 copy-start.2
  1206.5 18.7 slice-start.3
  1216.9 8.3 slice-start.4
  1242.3 148.1 %slice-start = ((s8[9437184]{0:T(1024)(128)(4,1)}), s8[4194304]{0:T(1024)(128)(4,1)S(1)}, s32[]{:S(2)}) async-start(s8[9437184]{0:T(1024)(128)(4,1)} %bitcast.463), calls=%async_computation.14 | async-start | bytes 8388608
  1242.3 148.1 %slice-start.1 = ((s8[9437184]{0:T(1024)(128)(4,1)}), s8[4194304]{0:T(1024)(128)(4,1)S(1)}, s32[]{:S(2)}) async-start(s8[9437184]{0:T(1024)(128)(4,1)} %bitcast.463), calls=%async_computation.15 | async-start | bytes 8388608
  1389.7 1.2 slice-start.2
  1495.0 5.4 copy-start.10
  1495.0 141.6 %all-to-all-start.6 = ((f32[4,48,64,128]{3,2,1,0:T(8,128)}), f32[4,48,64,128]{3,2,1,0:T(8,128)}, u32[]{:S(2)}, u32[]{:S(2)}) async-start(f32[4,48,64,128]{3,2,1,0:T(8,128)} %bitcast.471), calls=%async_computation.6 | async-start | bytes 12582912 | tf_op jit(solution)/shard_map/all_to_all | solution.py:100
  1636.6 25.3 %all-to-all-start.8 = ((f32[4,256,128]{2,1,0:T(8,128)}), f32[4,256,128]{2,1,0:T(8,128)S(1)}, u32[]{:S(2)}, u32[]{:S(2)}) async-start(f32[4,256,128]{2,1,0:T(8,128)} %broadcast_select_fusion), calls=%async_computation.8 | async-start | bytes 1048576 | tf_op jit(solution)/shard_map/all_to_all | solution.py:156
  1661.9 6.6 copy-start.4
  1661.9 11.1 copy-start.8
  1661.9 11.3 copy-start.9
  1661.9 0.8 copy-start.5
  1662.7 212.0 %all-to-all-start.7 = ((f32[4,192,24,128]{3,1,2,0:T(8,128)}), f32[4,192,24,128]{3,1,2,0:T(8,128)}, u32[]{:S(2)}, u32[]{:S(2)}) async-start(f32[4,192,24,128]{3,1,2,0:T(8,128)} %convolution_bitcast_fusion), calls=%async_computation.7 | async-start | bytes 18874368 | tf_op jit(solution)/shard_map/all_to_all | solution.py:100
  1668.5 17.9 all-gather.10.cloned.1.call-start
  1668.6 6.2 collective-permute-start
  1671.7 5.7 collective-permute-start.1
  1674.6 227.8 %all-gather.12.cloned.1.call-start = ((), (), s32[]{:S(2)}) async-start(), calls=%async_computation.12 | async-start | bytes 1572864 | tf_op jit(solution)/shard_map/all_gather | solution.py:112
  1677.5 0.8 copy-start.6
  1678.4 97.3 %collective-permute-start.3 = (f32[70,3,128]{2,1,0:T(4,128)S(1)}, f32[70,3,128]{2,1,0:T(4,128)}, u32[]{:S(2)}, u32[]{:S(2)}) collective-permute-start(f32[70,3,128]{2,1,0:T(4,128)S(1)} %get-tuple-element.547), channel_id=1, source_target_pairs={{2,0},{4,2},{6,4},{3,1},{5,3},{7,5},{10,8},{12,10},{14,12},{11,9},... | collective-permute-start | bytes 322568 | tf_op jit(solution)/shard_map/ppermute | solution.py:28
  1679.7 143.3 %collective-permute-start.2 = (f32[70,3,128]{2,1,0:T(4,128)S(1)}, f32[70,3,128]{2,1,0:T(4,128)}, u32[]{:S(2)}, u32[]{:S(2)}) collective-permute-start(f32[70,3,128]{2,1,0:T(4,128)S(1)} %get-tuple-element.546), channel_id=1, source_target_pairs={{0,2},{2,4},{4,6},{1,3},{3,5},{5,7},{8,10},{10,12},{12,14},{9,11},... | collective-permute-start | bytes 322568 | tf_op jit(solution)/shard_map/ppermute | solution.py:25
  1842.4 71.6 %all-gather.14.cloned.1.call-start = ((), (), s32[]{:S(2)}) async-start(), calls=%async_computation.13 | async-start | bytes 1572864 | tf_op jit(solution)/shard_map/all_gather | solution.py:112
  1843.0 108.0 %all-gather.8.cloned.1.call-start = ((), (), s32[]{:S(2)}) async-start(), calls=%async_computation.10 | async-start | bytes 28311552 | tf_op jit(solution)/shard_map/all_gather | solution.py:112
  1887.7 0.7 copy-start.11
  1887.7 1.0 copy-start.7
  1887.7 26.3 %copy-start.12 = (f32[256]{0:T(256)S(1)}, f32[256]{0:T(256)}, u32[]{:S(2)}) copy-start(f32[256]{0:T(256)} %param.25) | copy-start | bytes 3076
  1888.4 31.0 %copy-start.15 = (f32[128]{0:T(128)S(1)}, f32[128]{0:T(128)}, u32[]{:S(2)}) copy-start(f32[128]{0:T(128)} %param.28) | copy-start | bytes 1540
  1919.4 12.5 copy-start.13
  1933.0 70.5 %copy-start.14 = (f32[768,128]{1,0:T(8,128)S(1)}, f32[768,128]{1,0:T(8,128)}, u32[]{:S(2)}) copy-start(f32[768,128]{1,0:T(8,128)} %param.21) | copy-start | bytes 1179652
  2180.9 13.0 copy-start.1
Sparse Core Ops, SparseCore 0:
  1184.3 22.1 all-gather.5
  1674.7 11.6 all-gather.9
  1842.5 59.7 all-gather.11
  1903.8 10.2 all-gather.13
  1916.0 34.9 all-gather.7
where the time goes:
time: 2220 us; the launch traced here: 2200 us
  waiting for transfers between devices  694 us (31%)
  blocking collectives  367 us (17%)
  other arithmetic  358 us (16%)
  matrix products  356 us (16%)
  loops' own time  259 us (12%)
  local copies, waits for them, and re-layouts  109 us (5%)
  starting transfers between devices  43.3 us (2%)
    all_to_all x4, waiting for transfers between devices, regroup(): lax.all_to_all(blocks, 'lon', split_axis=0, concat_axis=2, tiled=True)[0]  498 us
    all_to_all x2, blocking collectives, degree_exchange(): lax.all_to_all(blocks, ('lat', 'lon'), split_axis=0, concat_axis=2, tiled...  291 us
    another operation x1, loops' own time, legendre_table(): lax.scan(advance, (zeros_grid, zeros_grid, zeros_grid), jnp.arange(degree...  259 us
    gt x384, other arithmetic, advance(): degree > orders[:, None]  248 us
    dot_general x2, matrix products, feed_forward(): jnp.dot(hidden, down_weight, precision=best_precision, preferred_element_...  190 us
    ppermute x2, waiting for transfers between devices, with_halo(): lax.ppermute(lax.slice_in_dim(block, 0, width, axis=dim), axis, backward)  86.7 us
    all_to_all x1, blocking collectives, band_exchange(): lax.all_to_all(blocks, 'lat', split_axis=0, concat_axis=2, tiled=True)  73.6 us
    all_gather x5, waiting for transfers between devices, channel_join(): return lax.all_gather(matrix, 'feat', axis=1, tiled=True)  61.3 us
  transfers between devices with their start and end apart: 15, of which 12 were waited for; matrix products, arithmetic and copies ran while one was open for 20% of the time, Pallas kernels for 0%

commit v1 on v0

--- a/solution.py
+++ b/solution.py
@@ -3,6 +3,8 @@
 import jax
 import jax.numpy as jnp
 from jax import lax
+from jax.experimental import pallas as pl
+from jax.experimental.pallas import tpu as pltpu
 from jax.sharding import PartitionSpec as P
 
 C = 256
@@ -14,7 +16,7 @@
 BLOCK = 8
 
 
-best_precision = lax.Precision.HIGHEST
+best_precision = lax.Precision.HIGH
 
 
 def with_halo(block, sides, width):
@@ -43,37 +45,66 @@
         jnp.where(steps_k[None, :] <= orders[:, None], log_terms[None, :], 0.0), axis=1
     )
     log_start = 0.5 * (math.log(0.5) + log_norm[:, None]) + order_f * jnp.log(sine)[None, :]
-    zeros_grid = jnp.zeros((orders.shape[0], lat_count), jnp.float32)
-
-    def advance(carry, degree):
-        current, previous, shift = carry
-        deg_f = degree.astype(jnp.float32)
-        order_sq = order_f * order_f
-        factor_a = jnp.sqrt(
-            jnp.maximum(4.0 * deg_f * deg_f - 1.0, 0.0) / jnp.maximum(deg_f * deg_f - order_sq, 1.0)
-        )
-        below = deg_f - 1.0
-        factor_b = jnp.sqrt(
-            jnp.maximum(below * below - order_sq, 0.0) / jnp.maximum(4.0 * below * below - 1.0, 1.0)
-        )
-        recurred = factor_a * (cosine[None, :] * current - factor_b * previous)
-        fresh = jnp.where(
-            degree == orders[:, None], 1.0, jnp.where(degree > orders[:, None], recurred, 0.0)
-        )
-        large = jnp.abs(fresh) > 2.0**32
-        rescale = jnp.where(large, 2.0 ** (-32), 1.0)
-        fresh = fresh * rescale
-        shift = shift + jnp.where(large, 32.0, 0.0)
-        value = fresh * jnp.exp(log_start + shift * math.log(2.0))
-        return ((fresh, current * rescale, shift), value)
-
-    final_state, table = lax.scan(
-        advance,
-        (zeros_grid, zeros_grid, zeros_grid),
-        jnp.arange(degree_count, dtype=jnp.int32),
-        unroll=16,
-    )
-    return table
+    degree_f = jnp.arange(degree_count, dtype=jnp.int32).astype(jnp.float32)[:, None, None]
+    order_sq = order_f * order_f
+    factor_a = jnp.sqrt(
+        jnp.maximum(4.0 * degree_f * degree_f - 1.0, 0.0)
+        / jnp.maximum(degree_f * degree_f - order_sq, 1.0)
+    )
+    below = degree_f - 1.0
+    factor_b = jnp.sqrt(
+        jnp.maximum(below * below - order_sq, 0.0) / jnp.maximum(4.0 * below * below - 1.0, 1.0)
+    )
+    count = orders.shape[0]
+    order_grid = jnp.broadcast_to(orders[:, None], (count, lat_count))
+    chunk = math.gcd(degree_count, 48)
+
+    def recur(start_ref, order_ref, cosine_ref, a_ref, b_ref, table_ref, state):
+        @pl.when(pl.program_id(0) == 0)
+        def _():
+            state[...] = jnp.zeros_like(state)
+
+        log_scale = start_ref[...]
+        order = order_ref[...]
+        cos_grid = cosine_ref[...]
+        first = pl.program_id(0) * chunk
+        current, previous, shift = state[0], state[1], state[2]
+        for step in range(chunk):
+            degree = first + step
+            recurred = a_ref[step] * (cos_grid * current - b_ref[step] * previous)
+            fresh = jnp.where(
+                degree == order, 1.0, jnp.where(degree > order, recurred, 0.0)
+            )
+            large = jnp.abs(fresh) > 2.0**32
+            rescale = jnp.where(large, 2.0 ** (-32), 1.0)
+            fresh = fresh * rescale
+            shift = shift + jnp.where(large, 32.0, 0.0)
+            table_ref[step] = fresh * jnp.exp(log_scale + shift * math.log(2.0))
+            current, previous = fresh, current * rescale
+        state[0], state[1], state[2] = current, previous, shift
+
+    whole = pl.BlockSpec((count, lat_count), lambda i: (0, 0))
+    factor = pl.BlockSpec((chunk, count, 1), lambda i: (i, 0, 0))
+    return pl.pallas_call(
+        recur,
+        grid=(degree_count // chunk,),
+        in_specs=[whole, whole, whole, factor, factor],
+        out_specs=pl.BlockSpec((chunk, count, lat_count), lambda i: (i, 0, 0)),
+        out_shape=jax.ShapeDtypeStruct((degree_count, count, lat_count), jnp.float32),
+        scratch_shapes=[pltpu.VMEM((3, count, lat_count), jnp.float32)],
+        compiler_params=pltpu.CompilerParams(vmem_limit_bytes=32 * 2**20),
+        cost_estimate=pl.CostEstimate(
+            flops=60 * degree_count * count * lat_count,
+            bytes_accessed=60 * degree_count * count * lat_count,
+            transcendentals=degree_count * count * lat_count,
+        ),
+    )(
+        log_start,
+        order_grid,
+        jnp.broadcast_to(cosine[None, :], (count, lat_count)),
+        factor_a,
+        factor_b,
+    )
 
 
 def quadrature(lat_ids, lat_count):
@@ -100,8 +131,61 @@
     return lax.all_to_all(blocks, "lon", split_axis=0, concat_axis=2, tiled=True)[0]
 
 
-def band_exchange(blocks):
-    return lax.all_to_all(blocks, "lat", split_axis=0, concat_axis=2, tiled=True)
+def split_value(value):
+    high = value.astype(jnp.bfloat16)
+    return high, (value - high.astype(jnp.float32)).astype(jnp.bfloat16)
+
+
+def split_dot(left, right_high, right_low):
+    left_high, left_low = split_value(left)
+
+    def part(one, other):
+        return jnp.dot(one, other, preferred_element_type=jnp.float32)
+
+    return part(left_high, right_high) + (
+        part(left_high, right_low) + part(left_low, right_high)
+    )
+
+
+def mlp_kernel(rows_ref, up_ref, down_ref, out_ref, up_high, up_low, down_high, down_low):
+    @pl.when(pl.program_id(0) == 0)
+    def _():
+        up_high[...], up_low[...] = split_value(up_ref[...])
+        down_high[...], down_low[...] = split_value(down_ref[...])
+
+    rows = rows_ref[...]
+    pre = split_dot(rows, up_high[...], up_low[...])
+    hidden = 0.5 * pre * (1.0 + lax.erf(pre * math.sqrt(0.5)))
+    out_ref[...] = rows + split_dot(hidden, down_high[...], down_low[...])
+
+
+def residual_mlp(rows, up, down):
+    count, width = rows.shape
+    middle = up.shape[1]
+    block = math.gcd(count, 512)
+    return pl.pallas_call(
+        mlp_kernel,
+        grid=(count // block,),
+        in_specs=[
+            pl.BlockSpec((block, width), lambda i: (i, 0)),
+            pl.BlockSpec((width, middle), lambda i: (0, 0)),
+            pl.BlockSpec((middle, width), lambda i: (0, 0)),
+        ],
+        out_specs=pl.BlockSpec((block, width), lambda i: (i, 0)),
+        out_shape=jax.ShapeDtypeStruct((count, width), jnp.float32),
+        scratch_shapes=[
+            pltpu.VMEM((width, middle), jnp.bfloat16),
+            pltpu.VMEM((width, middle), jnp.bfloat16),
+            pltpu.VMEM((middle, width), jnp.bfloat16),
+            pltpu.VMEM((middle, width), jnp.bfloat16),
+        ],
+        compiler_params=pltpu.CompilerParams(vmem_limit_bytes=40 * 2**20),
+        cost_estimate=pl.CostEstimate(
+            flops=12 * count * width * middle,
+            bytes_accessed=8 * count * width,
+            transcendentals=count * middle,
+        ),
+    )(rows, up, down)
 
 
 def degree_exchange(blocks):
@@ -147,10 +231,10 @@
     lat_index = lax.axis_index("lat")
     lon_index = lax.axis_index("lon")
     band_rows = lat_rows // lon_devices
-    order_local = MMAX // lon_devices
+    places = lat_devices * lon_devices
     degree_rows = LMAX // lat_devices
     mix_rows = degree_rows // lon_devices
-    few_orders = order_local // lat_devices
+    few_orders = MMAX // places
     flat_atm = atmosphere.reshape(-1, half_chan)
     picked = jnp.take(flat_atm, regrid_rows.reshape(-1), axis=0).reshape(lon_devices, -1, half_chan)
     arrived = lax.all_to_all(picked, "lon", split_axis=0, concat_axis=0, tiled=True)
@@ -158,16 +242,20 @@
     spectrum = jnp.einsum(
         "anc,rnm->mrac", grid, forward_table(NLON, MMAX), precision=best_precision
     )
-    spectrum = regroup(spectrum.reshape(lon_devices, order_local * 2, band_rows, half_chan))
-    spectrum = spectrum.reshape(order_local, 2, lat_rows, half_chan)
-    spread = band_exchange(spectrum)
-    orders = (
-        lon_index * order_local + lat_index * few_orders + jnp.arange(few_orders, dtype=jnp.int32)
+    spectrum = spectrum.reshape(places, few_orders, 2, band_rows, half_chan)
+    row_ids = (lat_index * lon_devices + lon_index) * band_rows + jnp.arange(
+        band_rows, dtype=jnp.int32
+    )
+    spectrum = spectrum * quadrature(row_ids, NLAT)[:, None]
+    spread = lax.all_to_all(
+        spectrum, ("lat", "lon"), split_axis=0, concat_axis=3, tiled=True
+    )[0]
+    orders = (lat_index * lon_devices + lon_index) * few_orders + jnp.arange(
+        few_orders, dtype=jnp.int32
     )
     table = legendre_table(orders, LMAX, NLAT, MMAX)
-    quad = quadrature(jnp.arange(NLAT, dtype=jnp.int32), NLAT)
     coeffs = jnp.einsum(
-        "lmj,mrjc->lrmc", table * quad[None, None, :], spread, precision=best_precision
+        "lmj,mrjc->lrmc", table, spread, precision=best_precision
     )
     mix_flat = degree_exchange(coeffs).reshape(-1, half_chan)
     mix_input = channel_join(mix_flat).reshape(mix_rows, 2, MMAX, C)
@@ -180,17 +268,39 @@
     mixed = jnp.stack([real_part, imag_part], axis=1)
     back = degree_exchange(mixed)
     full_modes = jnp.einsum("lmj,mrlc->jrmc", table, back, precision=best_precision)
-    grid_modes = band_exchange(full_modes)
-    wave_rows = regroup(grid_modes.reshape(lon_devices, band_rows * 2, order_local, half_chan))
-    wave_rows = wave_rows.reshape(band_rows, 2, MMAX, half_chan)
-    spatial = jnp.einsum(
-        "armc,rmn->nac", wave_rows, inverse_table(NLON, MMAX), precision=best_precision
-    )
-    spatial = regroup(spatial.reshape(lon_devices, lon_cols, band_rows, half_chan))
-    summed = atmosphere + jnp.transpose(spatial, (1, 0, 2))
-    full_input = channel_join(summed.reshape(-1, half_chan))
-    atm_update = feed_forward(full_input, mlp_in, mlp_out)
-    atmos_next = summed + atm_update.reshape(lat_rows, lon_cols, half_chan)
+    wave_rows = lax.all_to_all(
+        full_modes, ("lat", "lon"), split_axis=0, concat_axis=2, tiled=True
+    )
+    inverse = inverse_table(NLON, MMAX)
+    whole_in = channel_join(mlp_in)
+    whole_out = channel_join(mlp_out)
+    pieces = 3 if band_rows % 6 == 0 else 1
+    piece_rows = band_rows // pieces
+    row_axis = 0 if piece_rows % 2 == 0 else 1
+    finished = []
+    for piece in range(pieces):
+        span = slice(piece * piece_rows, (piece + 1) * piece_rows)
+        summed = grid[span] + jnp.einsum(
+            "armc,rmn->anc", wave_rows[span], inverse, precision=best_precision
+        )
+        full_input = lax.all_to_all(
+            summed, "feat", split_axis=row_axis, concat_axis=2, tiled=True
+        )
+        result = residual_mlp(full_input.reshape(-1, C), whole_in, whole_out)
+        result = lax.all_to_all(
+            result.reshape(full_input.shape), "feat", split_axis=2, concat_axis=row_axis, tiled=True
+        )
+        result = result.reshape(piece_rows, lon_devices, lon_cols, half_chan)
+        finished.append(
+            lax.all_to_all(
+                jnp.transpose(result, (1, 0, 2, 3)),
+                "lon",
+                split_axis=0,
+                concat_axis=0,
+                tiled=True,
+            )
+        )
+    atmos_next = jnp.concatenate(finished, axis=1).reshape(lat_rows, lon_cols, half_chan)
     tile_rows, tile_cols, ocean_half = ocean_state.shape
     padded = with_halo(ocean_state, (("lat", 0), ("lon", 1)), KERNEL // 2)
     conv = jnp.zeros((tile_rows, tile_cols, ocean_half), jnp.float32) + depth_bias

time: 2220 us -> 1410 us (0.64)
  other arithmetic: 358 us -> 57 us
  matrix products: 356 us -> 84.9 us
  loops' own time: 259 us -> 0 us
  waiting for transfers between devices: 694 us -> 636 us
  Pallas kernels: 0 us -> 50.2 us
  local copies, waits for them, and re-layouts: 109 us -> 149 us
  blocking collectives: 367 us -> 337 us
  starting transfers between devices: 43.3 us -> 65.9 us
    all_to_all x1 -> x6, waiting for transfers between devices: 0.01 us -> 365 us  [the longest x1 136 us: shards(): lax.all_to_all(spectrum, ('lat', 'lon'), split_axis=0, concat_axis=3, til...]
    all_to_all x4 -> x1, waiting for transfers between devices: 498 us -> 203 us  [regroup(): lax.all_to_all(blocks, 'lon', split_axis=0, concat_axis=2, tiled=True)[0]]
    another operation x1 -> x0, loops' own time: 259 us -> none  [legendre_table(): lax.scan(advance, (zeros_grid, zeros_grid, zeros_grid), jnp.arange(degree...]
    gt x384 -> x0, other arithmetic: 248 us -> none  [advance(): degree > orders[:, None]]
    dot_general x2 -> x1, matrix products: 190 us -> 10.9 us  [feed_forward(): jnp.dot(hidden, down_weight, precision=best_precision, preferred_element_...]
    ppermute x2, waiting for transfers between devices: 86.7 us -> 2.56 us  [with_halo(): lax.ppermute(lax.slice_in_dim(block, 0, width, axis=dim), axis, backward)]
    dot_general x2 -> x1, matrix products: 57.9 us -> 3.49 us  [feed_forward(): jnp.dot(inputs, whole_up, precision=best_precision, preferred_element_typ...]
    pallas_call x0 -> x4, Pallas kernels: none -> 50.2 us  [the longest x3 43.4 us: residual_mlp(): pl.pallas_call(mlp_kernel, grid=(count // block,), in_specs=[pl.BlockSpec...]
  transfers between devices with their start and end apart: 15 -> 16, of which waited for: 12 -> 10; matrix products, arithmetic and copies ran while one was open for 20% -> 10% of each run, Pallas kernels for 0% -> 3%
where the time goes in v1:
time: 1410 us; the launch traced here: 1390 us
  waiting for transfers between devices  636 us (45%)
  blocking collectives  337 us (24%)
  local copies, waits for them, and re-layouts  149 us (11%)
  matrix products  84.9 us (6%)
  starting transfers between devices  65.9 us (5%)
  other arithmetic  57 us (4%)
  Pallas kernels  50.2 us (4%)
  between operations  14.6 us (1%)
    all_to_all x2, blocking collectives, degree_exchange(): lax.all_to_all(blocks, ('lat', 'lon'), split_axis=0, concat_axis=2, tiled...  290 us
    all_to_all x1, waiting for transfers between devices, regroup(): lax.all_to_all(blocks, 'lon', split_axis=0, concat_axis=2, tiled=True)[0]  203 us
    all_to_all x1, waiting for transfers between devices, shards(): lax.all_to_all(spectrum, ('lat', 'lon'), split_axis=0, concat_axis=3, til...  136 us
    all_to_all x1, waiting for transfers between devices, shards(): lax.all_to_all(full_modes, ('lat', 'lon'), split_axis=0, concat_axis=2, t...  126 us
    all_to_all x3, waiting for transfers between devices, shards(): lax.all_to_all(jnp.transpose(result, (1, 0, 2, 3)), 'lon', split_axis=0,...  103 us
    pallas_call x3, Pallas kernels, residual_mlp(): pl.pallas_call(mlp_kernel, grid=(count // block,), in_specs=[pl.BlockSpec...  43.4 us
    ppermute x2, waiting for transfers between devices, with_halo(): lax.ppermute(lax.slice_in_dim(block, block.shape[dim] - width, None, axis...  32.5 us
    all_to_all x3, starting transfers between devices, shards(): lax.all_to_all(jnp.transpose(result, (1, 0, 2, 3)), 'lon', split_axis=0,...  31.9 us
  transfers between devices with their start and end apart: 16, of which 10 were waited for; matrix products, arithmetic and copies ran while one was open for 10% of the time, Pallas kernels for 3%

profile of v1, /device:TPU:0, one launch (start us, length us, event | category | flops | bytes accessed | tf_op | source)
XLA Modules:
  0.0 1394.4 jit_solution(14119276865506526588)
XLA Ops:
  7.2 6.5 all-to-all-start
  16.9 203.4 %all-to-all-done = f32[4,24,192,128]{3,2,1,0:T(8,128)} async-done(((f32[4,24,192,128]{3,2,1,0:T(8,128)}), f32[4,24,192,128]{3,2,1,0:T(8,128)}, u32[]{:S(2)}, u32[]{:S(2)}) %all-to-all-start) | async-done | bytes 9437216 | tf_op jit(solution)/shard_map/all_to_all | solution.py:131
  220.3 4.3 copy.200
  224.7 8.5 fusion.116
  233.1 6.8 copy_multiply_fusion
  240.0 4.9 all-to-all-start.1
  245.3 4.9 divide_sqrt_fusion
  250.4 6.8 shard_map.167
  257.2 3.7 copy-done.1
  260.9 136.0 %all-to-all-done.1 = f32[16,16,2,24,128]{4,3,2,1,0:T(8,128)} async-done(((f32[16,16,2,24,128]{4,3,2,1,0:T(8,128)}), f32[16,16,2,24,128]{4,3,2,1,0:T(8,128)}, u32[]{:S(2)}, u32[]{:S(2)}) %all-to-all-start.1) | async-done | bytes 6291488 | tf_op jit(solution)/shard_map/all_to_all | solution.py:250
  396.9 3.7 copy.202
  402.4 14.1 %fusion.75 = f32[384,2,16,128]{0,3,1,2:T(8,128)} fusion(f32[16,2,384,128]{3,2,1,0:T(8,128)S(1)} %bitcast.290, f32[384,16,384,1]{2,1,0,3:T(8,128)S(1)} %bitcast.273), kind=kOutput, calls=%fused_computation.137 | convolution fusion | flops 3623878656 | bytes 22020096 | tf_op jit(solution)/shard_map/lmj,mrjc->lrmc/dot_general | solution.py:257
  416.6 10.3 copy.207
  426.9 143.2 %all_to_all.188 = f32[384,2,16,128]{3,1,2,0:T(2,128)S(1)} all-to-all(f32[384,2,16,128]{3,1,2,0:T(2,128)} %copy.207), channel_id=1, replica_groups=mesh['lat'=4,'lon'=4,'feat'=2] {'lat','lon'}, dimensions={0} | all-to-all | bytes 12582912 | tf_op jit(solution)/shard_map/all_to_all | solution.py:192
  570.8 3.5 copy.209
  574.3 22.2 %all-gather.5.cloned.1.call-done = f32[12288,256]{1,0:T(8,128)} async-done(((f32[12288,128]{1,0:T(8,128)}), f32[12288,256]{1,0:T(8,128)}) %all-gather.5.cloned.1.call-update) | async-done | bytes 12582928 | tf_op jit(solution)/shard_map/all_gather | solution.py:196
  596.6 8.3 fusion.5
  604.9 6.6 fusion.4
  611.6 4.7 subtract_bitcast_fusion
  616.3 5.7 add_bitcast_fusion
  624.3 3.6 copy.212
  627.9 147.1 %all_to_all.189 = f32[256,2,24,128]{3,2,1,0:T(8,128)S(1)} all-to-all(f32[256,2,24,128]{3,2,1,0:T(8,128)S(1)} %copy.212), channel_id=1, replica_groups=mesh['lat'=4,'lon'=4,'feat'=2] {'lat','lon'}, dimensions={0} | all-to-all | bytes 12582912 | tf_op jit(solution)/shard_map/all_to_all | solution.py:192
  776.2 10.4 fusion.78
  786.7 10.3 copy.216
  797.0 4.8 all-to-all-start.4
  801.8 6.5 gather_fusion
  814.1 4.5 cosine_multiply_fusion
  818.6 4.4 fusion.317
  828.6 126.2 %all-to-all-done.4 = f32[384,2,16,128]{3,1,2,0:T(2,128)} async-done(((f32[384,2,16,128]{3,1,2,0:T(2,128)}), f32[384,2,16,128]{3,1,2,0:T(2,128)}, u32[]{:S(2)}, u32[]{:S(2)}) %all-to-all-start.4) | async-done | bytes 6291488 | tf_op jit(solution)/shard_map/all_to_all | solution.py:271
  966.1 6.7 all_to_all.190
  975.4 14.5 %shard_map.169 = f32[3072,256]{1,0:T(8,128)S(1)} custom-call(f32[3072,256]{1,0:T(8,128)S(1)} %bitcast.281, f32[256,768]{1,0:T(8,128)S(1)} %all_gather.19.up_ref, f32[768,256]{1,0:T(8,128)S(1)} %all_gather.20.down_ref), custom_call_target="tpu_custom_call" | custom-call | flops 7247757312 | bytes 6291456 | tf_op jit(solution)/shard_map/pallas_call | solution.py:166
  991.6 5.0 copy.227
  1002.1 7.3 all_to_all.191
  1009.4 5.4 all-to-all-start.9
  1014.8 4.3 copy.219
  1023.0 4.5 bitcast_add_fusion
  1027.5 10.4 all_to_all.192
  1037.9 3.7 all-to-all-start.14
  1043.5 14.4 %shard_map.168 = f32[3072,256]{1,0:T(8,128)S(1)} custom-call(f32[3072,256]{1,0:T(8,128)S(1)} %bitcast.277, f32[256,768]{1,0:T(8,128)S(1)} %all_gather.19.up_ref, f32[768,256]{1,0:T(8,128)S(1)} %all_gather.20.down_ref), custom_call_target="tpu_custom_call" | custom-call | flops 7247757312 | bytes 6291456 | tf_op jit(solution)/shard_map/pallas_call | solution.py:166
  1059.7 4.2 copy.228
  1063.8 3.7 copy.229
  1067.5 3.9 copy.230
  1071.4 5.0 copy.220
  1076.4 4.3 copy.233
  1081.0 14.5 %shard_map.170 = f32[3072,256]{1,0:T(8,128)S(1)} custom-call(f32[3072,256]{1,0:T(8,128)S(1)} %bitcast.279, f32[256,768]{1,0:T(8,128)S(1)} %all_gather.19.up_ref, f32[768,256]{1,0:T(8,128)S(1)} %all_gather.20.down_ref), custom_call_target="tpu_custom_call" | custom-call | flops 7247757312 | bytes 6291456 | tf_op jit(solution)/shard_map/pallas_call | solution.py:166
  1097.1 5.0 copy.234
  1102.1 10.6 all_to_all.193
  1112.7 7.3 all_to_all.194
  1120.0 5.1 all-to-all-start.10
  1125.1 4.2 copy.221
  1132.7 4.0 copy.223
  1136.8 59.5 %all-to-all-done.10 = f32[4,8,192,128]{3,2,1,0:T(8,128)} async-done(((f32[4,8,192,128]{3,2,1,0:T(8,128)}), f32[4,8,192,128]{3,2,1,0:T(8,128)}, u32[]{:S(2)}, u32[]{:S(2)}) %all-to-all-start.10) | async-done | bytes 3145760 | tf_op jit(solution)/shard_map/all_to_all | solution.py:295
  1196.2 4.7 all-to-all-start.7
  1208.9 4.5 collective-permute-start.2
  1221.8 32.5 %collective-permute-done.2 = f32[70,3,128]{2,1,0:T(4,128)} collective-permute-done((f32[70,3,128]{2,1,0:T(4,128)S(1)}, f32[70,3,128]{2,1,0:T(4,128)}, u32[]{:S(2)}, u32[]{:S(2)}) %collective-permute-start.2) | collective-permute-done | bytes 107552 | tf_op jit(solution)/shard_map/ppermute | solution.py:27
  1254.3 21.0 %fusion.143 = f32[64,16,128]{2,1,0:T(8,128)} fusion(f32[70,16,128]{2,1,0:T(8,128)} %copy-done.18, f32[70,3,128]{2,1,0:T(4,128)} %collective-permute-done.3, f32[70,3,128]{2,1,0:T(4,128)} %collective-permute-done.2, f32[67,16,128]{2,1,0:T(8,128)S(1)} %get-tuple-element.66, f32[67,16,128]{2,1,0:T(8,128)S(1)} %get-tuple-element.10, ...), kind=kLoop, calls=%fused_computation.244 | loop fusion | flops 18612224 | bytes 5533696 | tf_op jit(solution)/shard_map/add | solution.py:321
  1275.3 4.2 copy.235
  1279.5 3.6 copy.236
  1283.1 3.9 copy.237
  1287.0 22.1 %all-to-all-start.13 = ((f32[4,8,192,128]{3,2,1,0:T(8,128)}), f32[4,8,192,128]{3,2,1,0:T(8,128)}, u32[]{:S(2)}, u32[]{:S(2)}) async-start(f32[4,8,192,128]{3,2,1,0:T(8,128)} %copy.237), calls=%async_computation.13 | async-start | bytes 6291456 | tf_op jit(solution)/shard_map/all_to_all | solution.py:295
  1313.0 6.8 all-gather.11.cloned.1.call-done
  1323.4 10.9 fusion.120
  1335.3 43.7 %all-to-all-done.13 = f32[4,8,192,128]{3,2,1,0:T(8,128)} async-done(((f32[4,8,192,128]{3,2,1,0:T(8,128)}), f32[4,8,192,128]{3,2,1,0:T(8,128)}, u32[]{:S(2)}, u32[]{:S(2)}) %all-to-all-start.13) | async-done | bytes 3145760 | tf_op jit(solution)/shard_map/all_to_all | solution.py:295
  1379.0 8.7 pad_maximum_fusion
  (155 shorter events, 79.7 us)
Async XLA Ops:
  7.2 1316.2 %copy-start = (f32[1024,128]{1,0:T(8,128)S(1)}, f32[1024,128]{1,0:T(8,128)}, u32[]{:S(2)}) copy-start(f32[1024,128]{1,0:T(8,128)} %param.25) | copy-start | bytes 1572868
  7.2 213.2 %all-to-all-start = ((f32[4,24,192,128]{3,2,1,0:T(8,128)}), f32[4,24,192,128]{3,2,1,0:T(8,128)}, u32[]{:S(2)}, u32[]{:S(2)}) async-start(f32[4,24,192,128]{3,2,1,0:T(8,128)} %bitcast.297), calls=%async_computation | async-start | bytes 18874368 | tf_op jit(solution)/shard_map/all_to_all | solution.py:131
  240.0 157.0 %all-to-all-start.1 = ((f32[16,16,2,24,128]{4,3,2,1,0:T(8,128)}), f32[16,16,2,24,128]{4,3,2,1,0:T(8,128)}, u32[]{:S(2)}, u32[]{:S(2)}) async-start(f32[16,16,2,24,128]{4,3,2,1,0:T(8,128)} %copy_multiply_fusion), calls=%async_computation.1 | async-start | bytes 12582912 | tf_op jit(solution)/shard_map/all_to_all | solution.py:250
  244.8 351.7 %all-gather.5.cloned.1.call-start = ((), (), s32[]{:S(2)}) async-start(), calls=%async_computation.15 | async-start | bytes 18874368 | tf_op jit(solution)/shard_map/all_gather | solution.py:196
  257.2 3.7 copy-start.1
  396.9 5.5 copy-start.2
  574.3 37.3 %slice-start.3 = ((s8[6291456]{0:T(1024)(128)(4,1)}), s8[2097152]{0:T(1024)(128)(4,1)S(1)}, s32[]{:S(2)}) async-start(s8[6291456]{0:T(1024)(128)(4,1)} %bitcast.295), calls=%async_computation.22 | async-start | bytes 4194304
  596.6 8.3 copy-start.7
  596.6 15.0 %slice-start.4 = ((s8[6291456]{0:T(1024)(128)(4,1)}), s8[4194304]{0:T(1024)(128)(4,1)S(1)}, s32[]{:S(2)}) async-start(s8[6291456]{0:T(1024)(128)(4,1)} %bitcast.295), calls=%async_computation.23 | async-start | bytes 8388608
  627.9 147.9 %slice-start = ((s8[9437184]{0:T(1024)(128)(4,1)}), s8[4194304]{0:T(1024)(128)(4,1)S(1)}, s32[]{:S(2)}) async-start(s8[9437184]{0:T(1024)(128)(4,1)} %bitcast.274), calls=%async_computation.19 | async-start | bytes 8388608
  627.9 147.9 %slice-start.1 = ((s8[9437184]{0:T(1024)(128)(4,1)}), s8[4194304]{0:T(1024)(128)(4,1)S(1)}, s32[]{:S(2)}) async-start(s8[9437184]{0:T(1024)(128)(4,1)} %bitcast.274), calls=%async_computation.20 | async-start | bytes 8388608
  775.0 1.2 slice-start.2
  797.0 4.8 copy-start.24
  797.0 157.9 %all-to-all-start.4 = ((f32[384,2,16,128]{3,1,2,0:T(2,128)}), f32[384,2,16,128]{3,1,2,0:T(2,128)}, u32[]{:S(2)}, u32[]{:S(2)}) async-start(f32[384,2,16,128]{3,1,2,0:T(2,128)} %copy.216), calls=%async_computation.4 | async-start | bytes 12582912 | tf_op jit(solution)/shard_map/all_to_all | solution.py:271
  801.8 6.6 copy-start.19
  801.8 9.0 copy-start.20
  961.1 1.9 copy-start.10
  961.2 2.1 copy-start.11
  989.9 1.7 copy-start.6
  996.6 2.5 copy-start.9
  996.6 2.7 copy-start.12
  1009.4 18.1 %all-to-all-start.9 = ((f32[4,768,256]{1,0,2:T(4,128)}), f32[4,768,256]{1,0,2:T(4,128)}, u32[]{:S(2)}, u32[]{:S(2)}) async-start(f32[4,768,256]{1,0,2:T(4,128)} %copy.227), calls=%async_computation.9 | async-start | bytes 6291456 | tf_op jit(solution)/shard_map/all_to_all | solution.py:290
  1019.2 2.5 copy-start.15
  1019.2 3.6 copy-start.8
  1019.2 3.8 copy-start.13
  1037.9 64.2 %all-to-all-start.14 = ((f32[4,256,128]{2,1,0:T(8,128)}), f32[4,256,128]{2,1,0:T(8,128)S(1)}, u32[]{:S(2)}, u32[]{:S(2)}) async-start(f32[4,256,128]{2,1,0:T(8,128)} %broadcast_select_fusion), calls=%async_computation.14 | async-start | bytes 1048576 | tf_op jit(solution)/shard_map/all_to_all | solution.py:240
  1041.6 1.9 copy-start.3
  1057.9 1.7 copy-start.4
  1095.4 1.7 copy-start.5
  1102.1 17.9 %copy-start.17 = (f32[4,256,128]{2,1,0:T(8,128)}, f32[4,256,128]{2,1,0:T(8,128)S(1)}, u32[]{:S(2)}) copy-start(f32[4,256,128]{2,1,0:T(8,128)S(1)} %all-to-all-done.14) | copy-start | bytes 1572868
  1102.1 10.6 copy-start.14
  1120.0 76.2 %all-to-all-start.10 = ((f32[4,8,192,128]{3,2,1,0:T(8,128)}), f32[4,8,192,128]{3,2,1,0:T(8,128)}, u32[]{:S(2)}, u32[]{:S(2)}) async-start(f32[4,8,192,128]{3,2,1,0:T(8,128)} %copy.230), calls=%async_computation.10 | async-start | bytes 6291456 | tf_op jit(solution)/shard_map/all_to_all | solution.py:295
  1136.8 64.2 %copy-start.16 = (f32[64,16,128]{2,1,0:T(8,128)S(1)}, f32[64,16,128]{2,1,0:T(8,128)}, u32[]{:S(2)}) copy-start(f32[64,16,128]{2,1,0:T(8,128)} %param.20) | copy-start | bytes 1572868
  1136.8 66.8 %copy-start.22 = (s32[64,16]{0,1:T(8,128)S(1)}, s32[64,16]{0,1:T(8,128)}, u32[]{:S(2)}) copy-start(s32[64,16]{0,1:T(8,128)} %param.30) | copy-start | bytes 12292
  1136.8 67.0 %copy-start.23 = (f32[7,7,128]{2,1,0:T(8,128)S(1)}, f32[7,7,128]{2,1,0:T(8,128)}, u32[]{:S(2)}) copy-start(f32[7,7,128]{2,1,0:T(8,128)} %param.21) | copy-start | bytes 75268
  1136.8 80.4 %copy-start.21 = (f32[256,128]{1,0:T(8,128)S(1)}, f32[256,128]{1,0:T(8,128)}, u32[]{:S(2)}) copy-start(f32[256,128]{1,0:T(8,128)} %param.28) | copy-start | bytes 393220
  1196.2 90.8 %all-to-all-start.7 = ((f32[4,8,192,128]{3,2,1,0:T(8,128)}), f32[4,8,192,128]{3,2,1,0:T(8,128)}, u32[]{:S(2)}, u32[]{:S(2)}) async-start(f32[4,8,192,128]{3,2,1,0:T(8,128)} %copy.223), calls=%async_computation.7 | async-start | bytes 6291456 | tf_op jit(solution)/shard_map/all_to_all | solution.py:295
  1200.9 16.2 %all-gather.7.cloned.1.call-start = ((), (), s32[]{:S(2)}) async-start(), calls=%async_computation.16 | async-start | bytes 1572864 | tf_op jit(solution)/shard_map/all_gather | solution.py:196
  1201.0 4.3 collective-permute-start
  1202.3 5.7 collective-permute-start.1
  1205.1 104.9 %all-gather.9.cloned.1.call-start = ((), (), s32[]{:S(2)}) async-start(), calls=%async_computation.17 | async-start | bytes 1572864 | tf_op jit(solution)/shard_map/all_gather | solution.py:196
  1208.0 0.8 copy-start.18
  1208.9 45.4 %collective-permute-start.2 = (f32[70,3,128]{2,1,0:T(4,128)S(1)}, f32[70,3,128]{2,1,0:T(4,128)}, u32[]{:S(2)}, u32[]{:S(2)}) collective-permute-start(f32[70,3,128]{2,1,0:T(4,128)S(1)} %get-tuple-element.8), channel_id=1, source_target_pairs={{0,2},{2,4},{4,6},{1,3},{3,5},{5,7},{8,10},{10,12},{12,14},{9,11},... | collective-permute-start | bytes 322568 | tf_op jit(solution)/shard_map/ppermute | solution.py:27
  1213.3 40.9 %collective-permute-start.3 = (f32[70,3,128]{2,1,0:T(4,128)S(1)}, f32[70,3,128]{2,1,0:T(4,128)}, u32[]{:S(2)}, u32[]{:S(2)}) collective-permute-start(f32[70,3,128]{2,1,0:T(4,128)S(1)} %get-tuple-element.9), channel_id=1, source_target_pairs={{2,0},{4,2},{6,4},{3,1},{5,3},{7,5},{10,8},{12,10},{14,12},{11,9},... | collective-permute-start | bytes 322568 | tf_op jit(solution)/shard_map/ppermute | solution.py:30
  1287.0 22.7 %copy-start.25 = (s32[8,2]{0,1:T(2,128)S(1)}, s32[8,2]{0,1:T(2,128)}, u32[]{:S(2)}) copy-start(s32[8,2]{0,1:T(2,128)} %param.31) | copy-start | bytes 196
  1287.0 32.9 %copy-start.26 = (f32[256]{0:T(256)S(1)}, f32[256]{0:T(256)}, u32[]{:S(2)}) copy-start(f32[256]{0:T(256)} %param.23) | copy-start | bytes 3076
  1287.0 92.1 %all-to-all-start.13 = ((f32[4,8,192,128]{3,2,1,0:T(8,128)}), f32[4,8,192,128]{3,2,1,0:T(8,128)}, u32[]{:S(2)}, u32[]{:S(2)}) async-start(f32[4,8,192,128]{3,2,1,0:T(8,128)} %copy.237), calls=%async_computation.13 | async-start | bytes 6291456 | tf_op jit(solution)/shard_map/all_to_all | solution.py:295
  1309.1 10.7 all-gather.11.cloned.1.call-start
  1310.0 13.4 copy-start.28
  1323.4 11.0 copy-start.27
Sparse Core Ops, SparseCore 0:
  574.5 22.0 all-gather.4
  1205.2 11.8 all-gather.6
  1275.4 25.3 all-gather.8
  1311.2 8.6 all-gather.10

commit v2 on v1

--- a/solution.py
+++ b/solution.py
@@ -239,6 +239,8 @@
     picked = jnp.take(flat_atm, regrid_rows.reshape(-1), axis=0).reshape(lon_devices, -1, half_chan)
     arrived = lax.all_to_all(picked, "lon", split_axis=0, concat_axis=0, tiled=True)
     grid = regroup(atmosphere.reshape(lon_devices, band_rows, lon_cols, half_chan))
+    padded = with_halo(ocean_state, (("lat", 0), ("lon", 1)), KERNEL // 2)
+    grid, padded, arrived = lax.optimization_barrier((grid, padded, arrived))
     spectrum = jnp.einsum(
         "anc,rnm->mrac", grid, forward_table(NLON, MMAX), precision=best_precision
     )
@@ -271,38 +273,7 @@
     wave_rows = lax.all_to_all(
         full_modes, ("lat", "lon"), split_axis=0, concat_axis=2, tiled=True
     )
-    inverse = inverse_table(NLON, MMAX)
-    whole_in = channel_join(mlp_in)
-    whole_out = channel_join(mlp_out)
-    pieces = 3 if band_rows % 6 == 0 else 1
-    piece_rows = band_rows // pieces
-    row_axis = 0 if piece_rows % 2 == 0 else 1
-    finished = []
-    for piece in range(pieces):
-        span = slice(piece * piece_rows, (piece + 1) * piece_rows)
-        summed = grid[span] + jnp.einsum(
-            "armc,rmn->anc", wave_rows[span], inverse, precision=best_precision
-        )
-        full_input = lax.all_to_all(
-            summed, "feat", split_axis=row_axis, concat_axis=2, tiled=True
-        )
-        result = residual_mlp(full_input.reshape(-1, C), whole_in, whole_out)
-        result = lax.all_to_all(
-            result.reshape(full_input.shape), "feat", split_axis=2, concat_axis=row_axis, tiled=True
-        )
-        result = result.reshape(piece_rows, lon_devices, lon_cols, half_chan)
-        finished.append(
-            lax.all_to_all(
-                jnp.transpose(result, (1, 0, 2, 3)),
-                "lon",
-                split_axis=0,
-                concat_axis=0,
-                tiled=True,
-            )
-        )
-    atmos_next = jnp.concatenate(finished, axis=1).reshape(lat_rows, lon_cols, half_chan)
     tile_rows, tile_cols, ocean_half = ocean_state.shape
-    padded = with_halo(ocean_state, (("lat", 0), ("lon", 1)), KERNEL // 2)
     conv = jnp.zeros((tile_rows, tile_cols, ocean_half), jnp.float32) + depth_bias
     for tap_row in range(KERNEL):
         for tap_col in range(KERNEL):
@@ -335,6 +306,37 @@
     ocean_next = ocean_state + cell_mask[:, :, None] * layer_scale * update.reshape(
         tile_rows, tile_cols, ocean_half
     )
+    wave_rows, ocean_next = lax.optimization_barrier((wave_rows, ocean_next))
+    inverse = inverse_table(NLON, MMAX)
+    whole_in = channel_join(mlp_in)
+    whole_out = channel_join(mlp_out)
+    pieces = 3 if band_rows % 6 == 0 else 1
+    piece_rows = band_rows // pieces
+    row_axis = 0 if piece_rows % 2 == 0 else 1
+    finished = []
+    for piece in range(pieces):
+        span = slice(piece * piece_rows, (piece + 1) * piece_rows)
+        summed = grid[span] + jnp.einsum(
+            "armc,rmn->anc", wave_rows[span], inverse, precision=best_precision
+        )
+        full_input = lax.all_to_all(
+            summed, "feat", split_axis=row_axis, concat_axis=2, tiled=True
+        )
+        result = residual_mlp(full_input.reshape(-1, C), whole_in, whole_out)
+        result = lax.all_to_all(
+            result.reshape(full_input.shape), "feat", split_axis=2, concat_axis=row_axis, tiled=True
+        )
+        result = result.reshape(piece_rows, lon_devices, lon_cols, half_chan)
+        finished.append(
+            lax.all_to_all(
+                jnp.transpose(result, (1, 0, 2, 3)),
+                "lon",
+                split_axis=0,
+                concat_axis=0,
+                tiled=True,
+            )
+        )
+    atmos_next = jnp.concatenate(finished, axis=1).reshape(lat_rows, lon_cols, half_chan)
     return (atmos_next, ocean_next)
 
 

time: 1410 us -> 1360 us (0.965)
  blocking collectives: 337 us -> 408 us
  waiting for transfers between devices: 636 us -> 593 us
  local copies, waits for them, and re-layouts: 149 us -> 112 us
  starting transfers between devices: 65.9 us -> 48.3 us
  other arithmetic: 57 us -> 39.6 us
    all_to_all x0 -> x1, blocking collectives: none -> 73.5 us  [shards(): lax.all_to_all(jnp.transpose(result, (1, 0, 2, 3)), 'lon', split_axis=0,...]
    all_to_all x1, waiting for transfers between devices: 126 us -> 93 us  [shards(): lax.all_to_all(full_modes, ('lat', 'lon'), split_axis=0, concat_axis=2, t...]
    ppermute x2, waiting for transfers between devices: 32.5 us -> 5.77 us  [with_halo(): lax.ppermute(lax.slice_in_dim(block, block.shape[dim] - width, None, axis...]
    all_to_all x3 -> x2, starting transfers between devices: 31.9 us -> 8.4 us  [shards(): lax.all_to_all(jnp.transpose(result, (1, 0, 2, 3)), 'lon', split_axis=0,...]
    all_to_all x3 -> x2, waiting for transfers between devices: 103 us -> 120 us  [shards(): lax.all_to_all(jnp.transpose(result, (1, 0, 2, 3)), 'lon', split_axis=0,...]
    add x1, other arithmetic: 21 us -> 5.14 us  [shards(): joined = conv + forcing]
    slice x8 -> x0, local copies, waits for them, and re-layouts: 15.1 us -> none  [the longest x4 9.95 us: shards(): grid[span]]
  transfers between devices with their start and end apart: 16 -> 15, of which waited for: 10 -> 11; matrix products, arithmetic and copies ran while one was open for 10% -> 6% of each run, Pallas kernels for 3% -> 2%
where the time goes in v2:
time: 1360 us
  waiting for transfers between devices  593 us (44%)
  blocking collectives  408 us (30%)
  local copies, waits for them, and re-layouts  112 us (8%)
  matrix products  89.1 us (7%)
  Pallas kernels  50.2 us (4%)
  starting transfers between devices  48.3 us (4%)
  other arithmetic  39.6 us (3%)
  between operations  15.1 us (1%)
    all_to_all x2, blocking collectives, degree_exchange(): lax.all_to_all(blocks, ('lat', 'lon'), split_axis=0, concat_axis=2, tiled...  291 us
    all_to_all x1, waiting for transfers between devices, regroup(): lax.all_to_all(blocks, 'lon', split_axis=0, concat_axis=2, tiled=True)[0]  190 us
    all_to_all x1, waiting for transfers between devices, shards(): lax.all_to_all(spectrum, ('lat', 'lon'), split_axis=0, concat_axis=3, til...  138 us
    all_to_all x2, waiting for transfers between devices, shards(): lax.all_to_all(jnp.transpose(result, (1, 0, 2, 3)), 'lon', split_axis=0,...  120 us
    all_to_all x1, waiting for transfers between devices, shards(): lax.all_to_all(full_modes, ('lat', 'lon'), split_axis=0, concat_axis=2, t...  93 us
    all_to_all x1, blocking collectives, shards(): lax.all_to_all(jnp.transpose(result, (1, 0, 2, 3)), 'lon', split_axis=0,...  73.5 us
    pallas_call x3, Pallas kernels, residual_mlp(): pl.pallas_call(mlp_kernel, grid=(count // block,), in_specs=[pl.BlockSpec...  43.3 us
    all_gather x4, waiting for transfers between devices, channel_join(): return lax.all_gather(matrix, 'feat', axis=1, tiled=True)  42.7 us
  transfers between devices with their start and end apart: 15, of which 11 were waited for; matrix products, arithmetic and copies ran while one was open for 6% of the time, Pallas kernels for 2%

profile of v2, /device:TPU:0, one launch (start us, length us, event | category | flops | bytes accessed | tf_op | source)
XLA Modules:
  0.0 1355.0 jit_solution(13222691564386010239)
XLA Ops:
  7.2 6.5 all-to-all-start
  13.7 4.3 collective-permute-start
  19.4 6.5 gather_fusion
  26.9 3.2 sine_negate_fusion
  30.1 190.3 %all-to-all-done = f32[4,24,192,128]{3,2,1,0:T(8,128)} async-done(((f32[4,24,192,128]{3,2,1,0:T(8,128)}), f32[4,24,192,128]{3,2,1,0:T(8,128)}, u32[]{:S(2)}, u32[]{:S(2)}) %all-to-all-start) | async-done | bytes 9437216 | tf_op jit(solution)/shard_map/all_to_all | solution.py:131
  220.4 4.1 all-to-all-start.1
  224.7 3.9 collective-permute-start.2
  230.1 5.8 collective-permute-done.2
  237.6 8.6 copy.178
  246.2 10.5 fusion
  256.7 6.4 copy_multiply_fusion
  263.1 7.9 all-to-all-start.2
  271.7 4.9 divide_sqrt_fusion
  276.7 6.8 shard_map.167
  283.6 3.6 copy-done.2
  287.2 138.3 %all-to-all-done.2 = f32[16,16,2,24,128]{4,3,2,1,0:T(8,128)} async-done(((f32[16,16,2,24,128]{4,3,2,1,0:T(8,128)}), f32[16,16,2,24,128]{4,3,2,1,0:T(8,128)}, u32[]{:S(2)}, u32[]{:S(2)}) %all-to-all-start.2) | async-done | bytes 6291488 | tf_op jit(solution)/shard_map/all_to_all | solution.py:252
  425.4 3.7 copy.180
  430.9 14.1 %fusion.77 = f32[384,2,16,128]{0,3,1,2:T(8,128)} fusion(f32[16,2,384,128]{3,2,1,0:T(8,128)S(1)} %bitcast.290, f32[384,16,384,1]{2,1,0,3:T(8,128)S(1)} %bitcast.265), kind=kOutput, calls=%fused_computation.99 | convolution fusion | flops 3623878656 | bytes 22020096 | tf_op jit(solution)/shard_map/lmj,mrjc->lrmc/dot_general | solution.py:259
  445.0 10.3 copy.185
  455.3 143.5 %all_to_all.191 = f32[384,2,16,128]{3,1,2,0:T(2,128)S(1)} all-to-all(f32[384,2,16,128]{3,1,2,0:T(2,128)} %copy.185), channel_id=1, replica_groups=mesh['lat'=4,'lon'=4,'feat'=2] {'lat','lon'}, dimensions={0} | all-to-all | bytes 12582912 | tf_op jit(solution)/shard_map/all_to_all | solution.py:192
  599.5 3.5 copy.187
  603.1 22.2 %all-gather.5.cloned.1.call-done = f32[12288,256]{1,0:T(8,128)} async-done(((f32[12288,128]{1,0:T(8,128)}), f32[12288,256]{1,0:T(8,128)}) %all-gather.5.cloned.1.call-update) | async-done | bytes 12582928 | tf_op jit(solution)/shard_map/all_gather | solution.py:196
  625.3 8.3 fusion.7
  633.7 6.7 fusion.6
  640.3 4.7 subtract_bitcast_fusion
  645.1 5.6 add_bitcast_fusion
  653.0 3.6 copy.190
  656.7 147.1 %all_to_all.192 = f32[256,2,24,128]{3,2,1,0:T(8,128)S(1)} all-to-all(f32[256,2,24,128]{3,2,1,0:T(8,128)S(1)} %copy.190), channel_id=1, replica_groups=mesh['lat'=4,'lon'=4,'feat'=2] {'lat','lon'}, dimensions={0} | all-to-all | bytes 12582912 | tf_op jit(solution)/shard_map/all_to_all | solution.py:192
  805.0 10.5 fusion.80
  815.5 10.3 copy.194
  825.8 4.8 all-to-all-start.5
  832.2 11.1 all-gather.7.cloned.1.call-done
  848.0 5.1 select_add_fusion
  859.4 3.3 cosine_multiply_fusion
  866.5 8.6 all-gather.11.cloned.1.call-done
  875.2 3.5 fusion.136
  878.7 10.9 fusion.133
  890.7 93.0 %all-to-all-done.5 = f32[384,2,16,128]{3,1,2,0:T(2,128)} async-done(((f32[384,2,16,128]{3,1,2,0:T(2,128)}), f32[384,2,16,128]{3,1,2,0:T(2,128)}, u32[]{:S(2)}, u32[]{:S(2)}) %all-to-all-start.5) | async-done | bytes 6291488 | tf_op jit(solution)/shard_map/all_to_all | solution.py:273
  983.7 3.7 copy.195
  989.4 3.0 bitcast_add_fusion.1
  992.3 4.6 bitcast_add_fusion.2
  996.9 4.8 bitcast_add_fusion
  1001.7 6.2 all_to_all.193
  1011.8 14.4 %shard_map.169 = f32[3072,256]{1,0:T(8,128)S(1)} custom-call(f32[3072,256]{1,0:T(8,128)S(1)} %bitcast.271, f32[256,768]{1,0:T(8,128)S(1)} %copy-done.4, f32[768,256]{1,0:T(8,128)S(1)} %copy-done.7), custom_call_target="tpu_custom_call" | custom-call | flops 7247757312 | bytes 6291456 | tf_op jit(solution)/shard_map/pallas_call | solution.py:166
  1029.1 7.5 all_to_all.194
  1039.7 4.0 copy.209
  1043.7 6.5 all_to_all.195
  1054.0 14.4 %shard_map.168 = f32[3072,256]{1,0:T(8,128)S(1)} custom-call(f32[3072,256]{1,0:T(8,128)S(1)} %bitcast.273, f32[256,768]{1,0:T(8,128)S(1)} %copy-done.5, f32[768,256]{1,0:T(8,128)S(1)} %copy-done.8), custom_call_target="tpu_custom_call" | custom-call | flops 7247757312 | bytes 6291456 | tf_op jit(solution)/shard_map/pallas_call | solution.py:166
  1068.5 3.0 copy.201
  1071.4 7.5 all_to_all.196
  1079.0 5.3 all-to-all-start.7
  1088.1 14.4 %shard_map.170 = f32[3072,256]{1,0:T(8,128)S(1)} custom-call(f32[3072,256]{1,0:T(8,128)S(1)} %bitcast.269, f32[256,768]{1,0:T(8,128)S(1)} %copy-done.6, f32[768,256]{1,0:T(8,128)S(1)} %copy-done.9), custom_call_target="tpu_custom_call" | custom-call | flops 7247757312 | bytes 6291456 | tf_op jit(solution)/shard_map/pallas_call | solution.py:166
  1105.3 10.4 all_to_all.197
  1115.7 3.7 all-to-all-start.11
  1119.4 4.2 copy.202
  1123.5 3.7 copy.203
  1127.2 3.9 copy.204
  1131.1 59.4 %all-to-all-done.11 = f32[4,8,192,128]{3,2,1,0:T(8,128)S(1)} async-done(((f32[4,8,192,128]{3,2,1,0:T(8,128)}), f32[4,8,192,128]{3,2,1,0:T(8,128)S(1)}, u32[]{:S(2)}, u32[]{:S(2)}) %all-to-all-start.11) | async-done | bytes 3145760 | tf_op jit(solution)/shard_map/all_to_all | solution.py:331
  1190.6 4.7 all-to-all-start.8
  1195.3 4.2 copy.212
  1199.5 3.6 copy.213
  1205.1 60.6 %all-to-all-done.8 = f32[4,8,192,128]{3,2,1,0:T(8,128)} async-done(((f32[4,8,192,128]{3,2,1,0:T(8,128)}), f32[4,8,192,128]{3,2,1,0:T(8,128)}, u32[]{:S(2)}, u32[]{:S(2)}) %all-to-all-start.8) | async-done | bytes 3145760 | tf_op jit(solution)/shard_map/all_to_all | solution.py:331
  1265.8 73.5 %all_to_all.198 = f32[4,8,192,128]{3,2,1,0:T(8,128)} all-to-all(f32[4,8,192,128]{3,2,1,0:T(8,128)S(1)} %copy.214), channel_id=1, replica_groups=mesh['lat'=4,'lon'=4,'feat'=2] {'lon'}, dimensions={0} | all-to-all | bytes 6291456 | tf_op jit(solution)/shard_map/all_to_all | solution.py:331
  1339.3 8.7 pad_maximum_fusion
  (159 shorter events, 53.8 us)
Async XLA Ops:
  7.2 871.5 %copy-start = (f32[1024,128]{1,0:T(8,128)S(1)}, f32[1024,128]{1,0:T(8,128)}, u32[]{:S(2)}) copy-start(f32[1024,128]{1,0:T(8,128)} %param.25) | copy-start | bytes 1572868
  7.2 6.5 copy-start.13
  7.2 12.1 copy-start.19
  7.2 213.2 %all-to-all-start = ((f32[4,24,192,128]{3,2,1,0:T(8,128)}), f32[4,24,192,128]{3,2,1,0:T(8,128)}, u32[]{:S(2)}, u32[]{:S(2)}) async-start(f32[4,24,192,128]{3,2,1,0:T(8,128)} %bitcast.297), calls=%async_computation | async-start | bytes 18874368 | tf_op jit(solution)/shard_map/all_to_all | solution.py:131
  13.7 210.9 %collective-permute-start = (f32[3,16,128]{2,1,0:T(8,128)S(1)}, f32[3,16,128]{2,1,0:T(8,128)S(1)}, u32[]{:S(2)}, u32[]{:S(2)}) collective-permute-start(f32[3,16,128]{2,1,0:T(8,128)S(1)} %get-tuple-element.15), channel_id=1, source_target_pairs={{0,8},{8,16},{16,24},{1,9},{9,17},{17,25},{2,10},{10,18},{18,26},{... | collective-permute-start | bytes 73736 | tf_op jit(solution)/shard_map/ppermute | solution.py:27
  18.0 206.6 %collective-permute-start.1 = (f32[3,16,128]{2,1,0:T(8,128)S(1)}, f32[3,16,128]{2,1,0:T(8,128)S(1)}, u32[]{:S(2)}, u32[]{:S(2)}) collective-permute-start(f32[3,16,128]{2,1,0:T(8,128)S(1)} %get-tuple-element.14), channel_id=1, source_target_pairs={{8,0},{16,8},{24,16},{9,1},{17,9},{25,17},{10,2},{18,10},{26,18},{... | collective-permute-start | bytes 73736 | tf_op jit(solution)/shard_map/ppermute | solution.py:30
  220.4 25.8 %all-to-all-start.1 = ((f32[4,256,128]{2,1,0:T(8,128)}), f32[4,256,128]{2,1,0:T(8,128)}, u32[]{:S(2)}, u32[]{:S(2)}) async-start(f32[4,256,128]{2,1,0:T(8,128)} %broadcast_select_fusion), calls=%async_computation.1 | async-start | bytes 1048576 | tf_op jit(solution)/shard_map/all_to_all | solution.py:240
  224.7 11.2 collective-permute-start.2
  228.6 8.9 collective-permute-start.3
  263.1 162.3 %all-to-all-start.2 = ((f32[16,16,2,24,128]{4,3,2,1,0:T(8,128)}), f32[16,16,2,24,128]{4,3,2,1,0:T(8,128)}, u32[]{:S(2)}, u32[]{:S(2)}) async-start(f32[16,16,2,24,128]{4,3,2,1,0:T(8,128)} %copy_multiply_fusion), calls=%async_computation.2 | async-start | bytes 12582912 | tf_op jit(solution)/shard_map/all_to_all | solution.py:252
  271.0 354.4 %all-gather.5.cloned.1.call-start = ((), (), s32[]{:S(2)}) async-start(), calls=%async_computation.15 | async-start | bytes 18874368 | tf_op jit(solution)/shard_map/all_gather | solution.py:196
  283.6 3.6 copy-start.2
  425.4 5.5 copy-start.3
  625.3 8.3 copy-start.10
  625.3 15.0 %slice-start.6 = ((s8[6291456]{0:T(1024)(128)(4,1)}), s8[4194304]{0:T(1024)(128)(4,1)S(1)}, s32[]{:S(2)}) async-start(s8[6291456]{0:T(1024)(128)(4,1)} %bitcast.295), calls=%async_computation.25 | async-start | bytes 8388608
  633.7 6.7 slice-start.7
  656.6 147.9 %slice-start = ((s8[9437184]{0:T(1024)(128)(4,1)}), s8[4194304]{0:T(1024)(128)(4,1)S(1)}, s32[]{:S(2)}) async-start(s8[9437184]{0:T(1024)(128)(4,1)} %bitcast.266), calls=%async_computation.19 | async-start | bytes 8388608
  656.7 147.9 %slice-start.1 = ((s8[9437184]{0:T(1024)(128)(4,1)}), s8[4194304]{0:T(1024)(128)(4,1)S(1)}, s32[]{:S(2)}) async-start(s8[9437184]{0:T(1024)(128)(4,1)} %bitcast.266), calls=%async_computation.20 | async-start | bytes 8388608
  803.8 1.2 slice-start.2
  825.8 4.8 copy-start.17
  825.8 5.6 copy-start.18
  825.8 17.4 %copy-start.16 = (f32[256,128]{1,0:T(8,128)S(1)}, f32[256,128]{1,0:T(8,128)}, u32[]{:S(2)}) copy-start(f32[256,128]{1,0:T(8,128)} %param.28) | copy-start | bytes 393220
  825.8 157.8 %all-to-all-start.5 = ((f32[384,2,16,128]{3,1,2,0:T(2,128)}), f32[384,2,16,128]{3,1,2,0:T(2,128)}, u32[]{:S(2)}, u32[]{:S(2)}) async-start(f32[384,2,16,128]{3,1,2,0:T(2,128)} %copy.194), calls=%async_computation.5 | async-start | bytes 12582912 | tf_op jit(solution)/shard_map/all_to_all | solution.py:273
  830.6 12.6 all-gather.7.cloned.1.call-start
  831.4 32.1 %all-gather.9.cloned.1.call-start = ((), (), s32[]{:S(2)}) async-start(), calls=%async_computation.17 | async-start | bytes 1572864 | tf_op jit(solution)/shard_map/all_gather | solution.py:196
  832.1 15.7 %copy-start.20 = (f32[128]{0:T(128)S(1)}, f32[128]{0:T(128)}, u32[]{:S(2)}) copy-start(f32[128]{0:T(128)} %get-tuple-element.45) | copy-start | bytes 1540
  832.1 15.8 %copy-start.21 = (f32[128]{0:T(128)S(1)}, f32[128]{0:T(128)}, u32[]{:S(2)}) copy-start(f32[128]{0:T(128)} %get-tuple-element.46) | copy-start | bytes 1540
  832.1 15.8 %copy-start.22 = (f32[128]{0:T(128)S(1)}, f32[128]{0:T(128)}, u32[]{:S(2)}) copy-start(f32[128]{0:T(128)} %get-tuple-element.47) | copy-start | bytes 1540
  832.1 15.8 %copy-start.23 = (f32[128]{0:T(128)S(1)}, f32[128]{0:T(128)}, u32[]{:S(2)}) copy-start(f32[128]{0:T(128)} %get-tuple-element.48) | copy-start | bytes 1540
  832.1 15.8 %copy-start.24 = (f32[128]{0:T(128)S(1)}, f32[128]{0:T(128)}, u32[]{:S(2)}) copy-start(f32[128]{0:T(128)} %get-tuple-element.49) | copy-start | bytes 1540
  832.1 15.8 %copy-start.25 = (f32[128]{0:T(128)S(1)}, f32[128]{0:T(128)}, u32[]{:S(2)}) copy-start(f32[128]{0:T(128)} %get-tuple-element.50) | copy-start | bytes 1540
  832.2 15.8 %copy-start.26 = (f32[128]{0:T(128)S(1)}, f32[128]{0:T(128)}, u32[]{:S(2)}) copy-start(f32[128]{0:T(128)} %get-tuple-element.51) | copy-start | bytes 1540
  847.9 5.8 copy-start.27
  847.9 6.0 copy-start.14
  847.9 8.5 copy-start.15
  853.1 22.1 %copy-start.28 = (f32[256]{0:T(256)S(1)}, f32[256]{0:T(256)}, u32[]{:S(2)}) copy-start(f32[256]{0:T(256)} %param.23) | copy-start | bytes 3076
  853.1 22.0 %all-gather.11.cloned.1.call-start = ((), (), s32[]{:S(2)}) async-start(), calls=%async_computation.18 | async-start | bytes 1572864 | tf_op jit(solution)/shard_map/all_gather | solution.py:196
  862.6 16.0 %copy-start.30 = (f32[128]{0:T(128)S(1)}, f32[128]{0:T(128)}, u32[]{:S(2)}) copy-start(f32[128]{0:T(128)} %param.26) | copy-start | bytes 1540
  878.7 11.0 copy-start.29
  983.7 4.6 slice-start.3
  983.7 5.3 slice-start.4
  987.3 2.0 slice-start.5
  1010.4 1.1 copy-start.4
  1010.4 1.4 copy-start.7
  1039.7 4.0 copy-start.11
  1052.6 1.1 copy-start.5
  1052.7 1.4 copy-start.8
  1079.0 26.3 %all-to-all-start.7 = ((f32[4,768,256]{1,0,2:T(4,128)}), f32[4,768,256]{1,0,2:T(4,128)}, u32[]{:S(2)}, u32[]{:S(2)}) async-start(f32[4,768,256]{1,0,2:T(4,128)} %copy.201), calls=%async_computation.7 | async-start | bytes 6291456 | tf_op jit(solution)/shard_map/all_to_all | solution.py:326
  1086.7 1.1 copy-start.6
  1086.7 1.4 copy-start.9
  1115.7 74.9 %all-to-all-start.11 = ((f32[4,8,192,128]{3,2,1,0:T(8,128)}), f32[4,8,192,128]{3,2,1,0:T(8,128)S(1)}, u32[]{:S(2)}, u32[]{:S(2)}) async-start(f32[4,8,192,128]{3,2,1,0:T(8,128)} %copy.209), calls=%async_computation.11 | async-start | bytes 6291456 | tf_op jit(solution)/shard_map/all_to_all | solution.py:331
  1190.6 8.9 copy-start.12
  1190.6 75.2 %all-to-all-start.8 = ((f32[4,8,192,128]{3,2,1,0:T(8,128)}), f32[4,8,192,128]{3,2,1,0:T(8,128)}, u32[]{:S(2)}, u32[]{:S(2)}) async-start(f32[4,8,192,128]{3,2,1,0:T(8,128)} %copy.204), calls=%async_computation.8 | async-start | bytes 6291456 | tf_op jit(solution)/shard_map/all_to_all | solution.py:331
  1339.3 8.7 copy-start.1
Sparse Core Ops, SparseCore 0:
  603.2 22.0 all-gather.4
  833.0 10.1 all-gather.6
  853.2 10.1 all-gather.8
  864.9 10.2 all-gather.10
